TPU v7x, 32 devices: a whole 2x2x4 slice. The times are simulated.
32 devices in a mesh: occ: 8 (over y, x, core), vir: 4 (over z).
Axes of the slice: x: 2, y: 2, z: 4, core: 2. Of those that a mesh axis runs over, the one named last changes fastest.
Arguments:
- three_index: bfloat16 [2048, 128, 640], P(('occ', 'vir')), may hold values from -0.69921875 to 0.69921875
- virt_coeff: bfloat16 [640, 512], replicated, may hold values from -0.25 to 0.25
- metric_root: bfloat16 [2048, 2048], P(('occ', 'vir')), may hold values from -0.125 to 0.125
- owner_table: int32 [128], replicated, may hold values from 0 to 127, each once
- pair_order: int32 [4], replicated, may hold values from 0 to 7
- occ_energy: float32 [128], replicated, may hold values from -1.5 to -0.3
- vir_energy: float32 [512], replicated, may hold values from 0.1 to 2.5
Outputs:
- density: float32 [128, 512, 2048], P('occ', 'vir')
Inputs may be any that keep to these rules, and one draw needn't show every extreme that they name: `owner_table`: each orbital once.
All inputs are finite; a program needn't handle non-finite values.
Results may differ from a plain program's by a relative error of at most 0.0045.
Values may be sent and summed in bfloat16 or wider, within the bound.
A program may use at most 192 MiB of HBM per device.

v0:
```python
import jax
import jax.numpy as jnp
from jax import lax
from jax.sharding import PartitionSpec as P


def spread(value, axis, source):
    kept = jnp.where(lax.axis_index(axis) == source, value, 0).astype(value.dtype)
    return lax.psum(kept, axis)


def local(three_index, virt_coeff, metric_root, owner_table, pair_order, occ_energy, vir_energy):
    aux_rows, orbitals, atomic = three_index.shape
    virtuals = virt_coeff.shape[1]
    occ_size = lax.axis_size("occ")
    vir_size = lax.axis_size("vir")
    devices = occ_size * vir_size
    per_dev = orbitals // devices
    flat = jnp.dot(
        three_index.reshape(aux_rows * orbitals, atomic),
        virt_coeff,
        preferred_element_type=jnp.float32,
    )
    half = flat.astype(jnp.bfloat16).reshape(aux_rows, orbitals, virtuals)
    ordered = jnp.take(half, owner_table, axis=1)
    owned = lax.all_to_all(ordered, ("occ", "vir"), split_axis=1, concat_axis=0, tiled=True)
    fitted = jnp.einsum(
        "qp,pka->kaq",
        lax.all_gather(metric_root, ("occ", "vir"), axis=0, tiled=True),
        owned,
        preferred_element_type=jnp.float32,
    ).astype(jnp.bfloat16)
    sliced = lax.all_to_all(fitted, "vir", split_axis=1, concat_axis=0, tiled=True)
    group = sliced.shape[0]
    block = sliced.shape[1]
    one_hot = (owner_table[:, None] == jnp.arange(orbitals, dtype=jnp.int32)[None, :]).astype(
        jnp.float32
    )
    eps = jnp.dot(one_hot, occ_energy, precision=lax.Precision.HIGHEST)
    occ_idx = lax.axis_index("occ")
    vir_idx = lax.axis_index("vir")
    own_eps = lax.dynamic_slice_in_dim(eps, occ_idx * group, group, 0)
    block_eps = lax.dynamic_slice_in_dim(vir_energy, vir_idx * block, block, 0)
    steps = pair_order.shape[0]
    roots = [pair_order[step] for step in range(steps)]
    density = jnp.zeros((group, block, sliced.shape[2]), jnp.float32)
    for root in roots:
        partner = spread(fitted, "occ", root)
        partner_eps = lax.dynamic_slice_in_dim(
            eps, (root * vir_size + vir_idx) * per_dev, per_dev, 0
        )
        pair = jnp.einsum("iaq,kbq->ikab", sliced, partner, preferred_element_type=jnp.float32)
        denom = (
            own_eps[:, None, None, None]
            + partner_eps[None, :, None, None]
            - block_eps[None, None, :, None]
            - vir_energy[None, None, None, :]
        )
        amp = (pair / denom).astype(jnp.bfloat16)
        density = density + jnp.einsum(
            "ikab,kbq->iaq", amp, partner, preferred_element_type=jnp.float32
        )
    return density


def solution(mesh):
    placed = (P(("occ", "vir"), None, None), P(), P(("occ", "vir"), None), P(), P(), P(), P())
    return jax.shard_map(
        local, mesh=mesh, in_specs=placed, out_specs=P("occ", "vir", None), check_vma=False
    )
```

profile of v0, /device:TPU:0, one launch (start us, length us, event | category | flops | bytes accessed | tf_op | source)
XLA Modules:
  0.0 920.3 jit_solution(6500617904932669056)
XLA Ops:
  6.5 0.0 copy-start
  6.5 0.7 compare_and_fusion
  7.3 0.7 compare_select_fusion
  7.9 0.0 copy-done
  7.9 12.9 %convolution_convert_fusion = bf16[8192,512]{1,0:T(8,128)(2,1)} fusion(bf16[8192,640]{1,0:T(8,128)(2,1)} %bitcast.106, bf16[640,512]{1,0:T(8,128)(2,1)S(1)} %copy-done), kind=kOutput, calls=%fused_computation.12 | convolution fusion | flops 5372903424 | bytes 19529728 | tf_op jit(solution)/shard_map/dot_general | solution.py:19
  20.9 11.4 %copy.21 = bf16[64,128,512]{2,0,1:T(8,128)(2,1)} copy(bf16[64,128,512]{2,1,0:T(8,128)(2,1)} %bitcast.105) | data formatting | bytes 16777216 | tf_op jit(solution)/shard_map/reshape | solution.py:24
  32.3 10.1 %gather_fusion = bf16[128,64,512]{2,1,0:T(8,128)(2,1)} fusion(bf16[64,128,512]{2,0,1:T(8,128)(2,1)} %copy.21, s32[1024]{0:T(1024)S(1)} %pad_clamp_fusion), kind=kCustom, calls=%fused_computation | custom fusion | bytes 16777728 | tf_op jit(solution)/shard_map/jit(_take)/gather | solution.py:25
  42.4 7.6 select_bitcast_fusion
  50.0 7.4 all-to-all-start
  57.4 0.0 all-gather.2.cloned.1.call-start
  57.5 0.7 all-gather.2.cloned.1.call-update
  58.1 0.3 all-reduce.3.cloned.1.call-start
  58.4 0.0 copy-done.5
  58.4 0.7 fusion.26
  61.6 215.7 %all-to-all-done = bf16[64,128,512]{2,0,1:T(8,128)(2,1)} async-done(((bf16[64,128,512]{2,0,1:T(8,128)(2,1)}), bf16[64,128,512]{2,0,1:T(8,128)(2,1)}, u32[]{:S(2)}, u32[]{:S(2)}) %all-to-all-start) | async-done | bytes 8388640 | tf_op jit(solution)/shard_map/all_to_all | solution.py:26
  277.3 7.9 copy.22
  285.2 27.1 %broadcast_select_fusion.3 = (bf16[4,512,2048]{2,1,0:T(8,128)(2,1)}, bf16[4,512,2048]{2,1,0:T(8,128)(2,1)}, bf16[4,512,2048]{2,1,0:T(8,128)(2,1)}, bf16[4,512,2048]{2,1,0:T(8,128)(2,1)}, bf16[4,512,2048]{2,1,0:T(8,128)(2,1)}) fusion(pred[]{:T(512)S(6)} %eq.25, pred[]{:T(512)S(6)} %eq.31, pred[]{:T(512)S(6)} %eq.30, pred[]{:T(512)S(6)} %eq.29, ...), kind=kOutput, calls=%fused_computation.31 | convolution fusion | flops 17200840704 | bytes 58720260 | tf_op jit(solution)/shard_map/qp,pka->kaq/dot_general | solution.py:27
  312.3 0.0 all-reduce.3.cloned.1.call-update
  312.3 12.1 %copy.24 = bf16[4,512,2048]{2,0,1:T(4,128)(2,1)} copy(bf16[4,512,2048]{2,1,0:T(8,128)(2,1)} %get-tuple-element.29) | data formatting | bytes 16777216 | tf_op jit(solution)/shard_map/convert_element_type | solution.py:32
  324.5 7.5 all-to-all-start.1
  334.5 0.0 copy-done.7
  334.5 0.1 dynamic_slice.20
  334.6 0.0 copy-done.8
  334.6 0.0 copy-done.9
  334.6 0.2 convolution_bitcast_fusion
  334.8 0.1 dynamic_slice.18
  334.9 0.1 fusion.25
  335.0 0.1 broadcast_add_fusion.3
  335.1 0.8 broadcast_subtract_fusion.3
  335.9 181.4 %all-to-all-done.1 = bf16[4,512,2048]{2,0,1:T(4,128)(2,1)} async-done(((bf16[4,512,2048]{2,0,1:T(4,128)(2,1)}), bf16[4,512,2048]{2,0,1:T(4,128)(2,1)}, u32[]{:S(2)}, u32[]{:S(2)}) %all-to-all-start.1) | async-done | bytes 8388640 | tf_op jit(solution)/shard_map/all_to_all | solution.py:33
  517.3 11.4 %copy.25 = bf16[4,512,2048]{2,1,0:T(8,128)(2,1)} copy(bf16[4,512,2048]{2,0,1:T(4,128)(2,1)} %all-to-all-done.1) | data formatting | bytes 16777216 | tf_op jit(solution)/shard_map/all_to_all | solution.py:33
  528.7 8.7 copy.26
  537.4 179.5 %all-reduce.3.cloned.1.call-done = (bf16[4,512,2048]{2,1,0:T(8,128)(2,1)}, bf16[4,512,2048]{2,1,0:T(8,128)(2,1)}, bf16[4,512,2048]{2,1,0:T(8,128)(2,1)}, bf16[4,512,2048]{2,1,0:T(8,128)(2,1)}) async-done(((bf16[4,512,2048]{2,1,0:T(8,128)(2,1)}, bf16[4,512,2048]{2,1,0:T(8,128)(2,1)}, bf16[4,512,2048]{2,1,0:T(8,128)(2,1)}, bf16[4,512,2048]{2,1,0:T(8,128)(2,1)}), (bf16[4,512,2048]{2,1,0:T(8,128)(2,1)}, ...) | async-done | bytes 33554448 | tf_op jit(solution)/shard_map/psum | solution.py:9
  716.9 23.1 %fusion = bf16[16,4,128,512]{2,3,1,0:T(8,128)(2,1)} fusion(bf16[16,128,2048,1]{2,1,3,0:T(8,128)(2,1)} %bitcast.100, bf16[4,512,2048]{2,1,0:T(8,128)(2,1)} %get-tuple-element.5, f32[16,4,128]{2,1,0:T(4,128)S(1)} %get-tuple-element.16, f32[512]{0:T(512)S(1)} %copy-done.7), kind=kOutput, calls=%fused_computation.3 | convolution fusion | flops 17192452096 | bytes 25200640 | tf_op jit(solution)/shard_map/iaq,kbq->ikab/dot_general | solution.py:52
  740.0 24.7 %fusion.4 = f32[16,128,2048,1]{2,1,3,0:T(8,128)} fusion(bf16[16,4,128,512]{2,3,1,0:T(8,128)(2,1)} %fusion, bf16[4,512,2048]{2,1,0:T(8,128)(2,1)} %get-tuple-element.5), kind=kOutput, calls=%fused_computation.13 | convolution fusion | flops 17179869184 | bytes 33554432 | tf_op jit(solution)/shard_map/ikab,kbq->iaq/dot_general | solution.py:60
  764.7 0.0 copy-done.2
  764.7 0.0 copy-done.6
  764.7 21.4 %fusion.1 = bf16[16,4,128,512]{2,3,1,0:T(8,128)(2,1)} fusion(bf16[16,128,2048,1]{2,1,3,0:T(8,128)(2,1)S(1)} %bitcast.101, bf16[4,512,2048]{2,1,0:T(8,128)(2,1)S(1)} %copy-done.6, f32[16,4,128]{2,1,0:T(4,128)S(1)} %get-tuple-element.15, f32[512]{0:T(512)S(1)} %copy-done.7), kind=kOutput, calls=%fused_computation.6 | convolution fusion | flops 17192452096 | bytes 25200640 | tf_op jit(solution)/shard_map/iaq,kbq->ikab/dot_general | solution.py:52
  786.0 24.7 %fusion.7 = f32[16,128,2048,1]{2,1,3,0:T(8,128)} fusion(bf16[16,4,128,512]{2,3,1,0:T(8,128)(2,1)} %fusion.1, bf16[4,512,2048]{2,1,0:T(8,128)(2,1)} %get-tuple-element.6), kind=kOutput, calls=%fused_computation.16 | convolution fusion | flops 17179869184 | bytes 33554432 | tf_op jit(solution)/shard_map/ikab,kbq->iaq/dot_general | solution.py:60
  810.8 0.0 copy-done.4
  810.8 22.0 %fusion.2 = bf16[16,4,128,512]{2,3,1,0:T(8,128)(2,1)} fusion(bf16[16,128,2048,1]{2,1,3,0:T(8,128)(2,1)S(1)} %bitcast.102, bf16[4,512,2048]{2,1,0:T(8,128)(2,1)} %get-tuple-element.7, f32[16,4,128]{2,1,0:T(4,128)S(1)} %copy-done.4, f32[512]{0:T(512)S(1)} %copy-done.7), kind=kOutput, calls=%fused_computation.9 | convolution fusion | flops 17192452096 | bytes 25200640 | tf_op jit(solution)/shard_map/iaq,kbq->ikab/dot_general | solution.py:52
  832.8 24.4 %fusion.10 = f32[16,128,2048,1]{2,1,3,0:T(8,128)} fusion(bf16[16,4,128,512]{2,3,1,0:T(8,128)(2,1)} %fusion.2, bf16[4,512,2048]{2,1,0:T(8,128)(2,1)} %get-tuple-element.7), kind=kOutput, calls=%fused_computation.19 | convolution fusion | flops 17179869184 | bytes 33554432 | tf_op jit(solution)/shard_map/ikab,kbq->iaq/dot_general | solution.py:60
  857.1 0.0 slice-done
  857.1 0.0 slice-done.1
  857.1 0.0 copy-done.3
  857.1 21.6 %fusion.3 = bf16[16,4,128,512]{2,3,1,0:T(8,128)(2,1)} fusion(bf16[16,128,2048,1]{2,1,3,0:T(8,128)(2,1)S(1)} %bitcast.103, bf16[4,512,2048]{2,1,0:T(8,128)(2,1)S(1)} %bitcast.99, f32[512]{0:T(512)S(1)} %copy-done.7, f32[16,4,128]{2,1,0:T(4,128)S(1)} %copy-done.3), kind=kOutput, calls=%fused_computation.11 | convolution fusion | flops 17192452096 | bytes 25200640 | tf_op jit(solution)/shard_map/iaq,kbq->ikab/dot_general | solution.py:52
  878.8 34.3 %bitcast_add_fusion = f32[16,128,2048]{2,1,0:T(8,128)} fusion(f32[16,128,2048,1]{2,1,3,0:T(8,128)} %fusion.4, f32[16,128,2048,1]{2,1,3,0:T(8,128)} %fusion.7, f32[16,128,2048,1]{2,1,3,0:T(8,128)} %fusion.10, bf16[16,4,128,512]{2,3,1,0:T(8,128)(2,1)} %fusion.3, bf16[4,512,2048]{2,1,0:T(8,128)(2,1)} %get-tuple-element.8), kind=kOutput, calls=%fused_computation.1 | convolution fusion | flops 17192452096 | bytes 83886080 | tf_op jit(solution)/shard_map/ikab,kbq->iaq/dot_general | solution.py:60
  913.0 0.0 copy-done.1
  (14 shorter events, 0.0 us)
Async XLA Ops:
  6.5 1.4 copy-start
  50.0 8.4 copy-start.5
  50.0 227.3 %all-to-all-start = ((bf16[64,128,512]{2,0,1:T(8,128)(2,1)}), bf16[64,128,512]{2,0,1:T(8,128)(2,1)}, u32[]{:S(2)}, u32[]{:S(2)}) async-start(bf16[64,128,512]{2,0,1:T(8,128)(2,1)} %select_bitcast_fusion), calls=%async_computation | async-start | bytes 16777216 | tf_op jit(solution)/shard_map/all_to_all | solution.py:26
  57.4 227.8 %all-gather.2.cloned.1.call-start = ((), (), s32[]{:S(2)}) async-start(), calls=%async_computation.2 | async-start | bytes 8650752 | tf_op jit(solution)/shard_map/all_gather | solution.py:29
  58.1 658.7 %all-reduce.3.cloned.1.call-start = ((), (), s32[]{:S(2)}) async-start(), calls=%async_computation.3 | async-start | bytes 67108864 | tf_op jit(solution)/shard_map/psum | solution.py:9
  324.5 10.0 %copy-start.7 = (f32[512]{0:T(512)S(1)}, f32[512]{0:T(512)}, u32[]{:S(2)}) copy-start(f32[512]{0:T(512)} %param.13) | copy-start | bytes 6148
  324.5 10.1 %copy-start.8 = (s32[128]{0:T(128)S(1)}, s32[128]{0:T(128)}, u32[]{:S(2)}) copy-start(s32[128]{0:T(128)} %param.10) | copy-start | bytes 1540
  324.5 10.1 %copy-start.9 = (f32[128]{0:T(128)S(1)}, f32[128]{0:T(128)}, u32[]{:S(2)}) copy-start(f32[128]{0:T(128)} %param.12) | copy-start | bytes 1540
  324.5 192.8 %all-to-all-start.1 = ((bf16[4,512,2048]{2,0,1:T(4,128)(2,1)}), bf16[4,512,2048]{2,0,1:T(4,128)(2,1)}, u32[]{:S(2)}, u32[]{:S(2)}) async-start(bf16[4,512,2048]{2,0,1:T(4,128)(2,1)} %copy.24), calls=%async_computation.1 | async-start | bytes 16777216 | tf_op jit(solution)/shard_map/all_to_all | solution.py:33
  740.0 24.7 %copy-start.2 = (bf16[4,4,128,2048]{3,2,1,0:T(8,128)(2,1)S(1)}, bf16[4,4,128,2048]{3,2,1,0:T(8,128)(2,1)}, u32[]{:S(2)}) copy-start(bf16[4,4,128,2048]{3,2,1,0:T(8,128)(2,1)} %copy.26) | copy-start | bytes 25165828
  740.0 24.7 %copy-start.6 = (bf16[4,512,2048]{2,1,0:T(8,128)(2,1)S(1)}, bf16[4,512,2048]{2,1,0:T(8,128)(2,1)}, u32[]{:S(2)}) copy-start(bf16[4,512,2048]{2,1,0:T(8,128)(2,1)} %get-tuple-element.6) | copy-start | bytes 25165828
  786.0 24.7 %copy-start.4 = (f32[16,4,128]{2,1,0:T(4,128)S(1)}, f32[16,4,128]{2,1,0:T(4,128)}, u32[]{:S(2)}) copy-start(f32[16,4,128]{2,1,0:T(4,128)} %get-tuple-element.14) | copy-start | bytes 98308
  786.0 71.1 %slice-start = ((s8[8388608]{0:T(1024)(128)(4,1)}), s8[4194304]{0:T(1024)(128)(4,1)S(1)}, s32[]{:S(2)}) async-start(s8[8388608]{0:T(1024)(128)(4,1)} %bitcast.98), calls=%async_computation.4 | async-start | bytes 8388608
  810.8 46.4 %slice-start.1 = ((s8[8388608]{0:T(1024)(128)(4,1)}), s8[4194304]{0:T(1024)(128)(4,1)S(1)}, s32[]{:S(2)}) async-start(s8[8388608]{0:T(1024)(128)(4,1)} %bitcast.98), calls=%async_computation.5 | async-start | bytes 8388608
  832.8 24.4 %copy-start.3 = (f32[16,4,128]{2,1,0:T(4,128)S(1)}, f32[16,4,128]{2,1,0:T(4,128)}, u32[]{:S(2)}) copy-start(f32[16,4,128]{2,1,0:T(4,128)} %get-tuple-element.13) | copy-start | bytes 98308
  878.8 34.3 %copy-start.1 = (bf16[640,512]{1,0:T(8,128)(2,1)S(1)}, bf16[640,512]{1,0:T(8,128)(2,1)}, u32[]{:S(2)}) copy-start(bf16[640,512]{1,0:T(8,128)(2,1)} %param.8) | copy-start | bytes 1966084
Sparse Core Ops, SparseCore 0:
  61.2 152.8 all-gather.1
  312.4 404.3 all-reduce.2
where the time goes:
time: 929 us; the launch traced here: 920 us
  waiting for transfers between devices  577 us (62%)
  matrix products  236 us (25%)
  local copies, waits for them, and re-layouts  62.7 us (7%)
  between operations  19 us (2%)
  starting transfers between devices  15.2 us (2%)
  other arithmetic  9.82 us (1%)
    all_to_all x1, waiting for transfers between devices, local(): lax.all_to_all(ordered, ('occ', 'vir'), split_axis=1, concat_axis=0, tile...  216 us
    all_to_all x1, waiting for transfers between devices, local(): lax.all_to_all(fitted, 'vir', split_axis=1, concat_axis=0, tiled=True)  181 us
    psum x1, waiting for transfers between devices, spread(): return lax.psum(kept, axis)  179 us
    dot_general x4, matrix products, local(): jnp.einsum('ikab,kbq->iaq', amp, partner, preferred_element_type=jnp.floa...  108 us
    dot_general x4, matrix products, local(): jnp.einsum('iaq,kbq->ikab', sliced, partner, preferred_element_type=jnp.f...  88.1 us
    dot_general x1, matrix products, local(): jnp.einsum('qp,pka->kaq', lax.all_gather(metric_root, ('occ', 'vir'), axi...  27.1 us
    all_to_all x2, local copies, waits for them, and re-layouts, local(): lax.all_to_all(fitted, 'vir', split_axis=1, concat_axis=0, tiled=True)  20.1 us
  transfers between devices with their start and end apart: 4, of which 3 were waited for; matrix products, arithmetic and copies ran while one was open for 5% of the time, Pallas kernels for 0%

commit v1 on v0

v1 whole, which is shorter than its diff:
```python
import functools

import jax
import jax.numpy as jnp
from jax import lax
from jax.experimental import pallas as pl
from jax.experimental.pallas import tpu as pltpu
from jax.sharding import PartitionSpec as P

AXES = ("occ", "vir")
CHUNKS = 4
PARTS = 2
VMEM = 50 * 1024 * 1024


def half_body(x_ref, coeff_ref, perm_ref, out_ref):
    rows, orbitals, atomic = x_ref.shape
    half = jnp.dot(
        x_ref[...].reshape(rows * orbitals, atomic),
        coeff_ref[...],
        preferred_element_type=jnp.float32,
    ).astype(jnp.bfloat16)
    for row in range(rows):
        out_ref[row] = jnp.dot(
            perm_ref[...],
            half[row * orbitals : (row + 1) * orbitals],
            preferred_element_type=jnp.float32,
        ).astype(jnp.bfloat16)


def half_step(three_index, virt_coeff, perm):
    aux_rows, orbitals, atomic = three_index.shape
    virtuals = virt_coeff.shape[1]
    rows = min(8, aux_rows)
    return pl.pallas_call(
        half_body,
        grid=(aux_rows // rows,),
        in_specs=[
            pl.BlockSpec((rows, orbitals, atomic), lambda i: (i, 0, 0)),
            pl.BlockSpec((atomic, virtuals), lambda i: (0, 0)),
            pl.BlockSpec((orbitals, orbitals), lambda i: (0, 0)),
        ],
        out_specs=pl.BlockSpec((rows, orbitals, virtuals), lambda i: (i, 0, 0)),
        out_shape=jax.ShapeDtypeStruct((aux_rows, orbitals, virtuals), jnp.bfloat16),
        compiler_params=pltpu.CompilerParams(vmem_limit_bytes=VMEM),
        cost_estimate=pl.CostEstimate(
            flops=2 * aux_rows * orbitals * virtuals * (atomic + orbitals),
            bytes_accessed=2 * aux_rows * orbitals * (atomic + virtuals),
            transcendentals=0,
        ),
        name="half",
    )(three_index, virt_coeff, perm)


def pair_body(count, carried, own_ref, row_ref, cols_ref, *refs):
    partners = refs[:count]
    out_ref = refs[-1]

    @pl.when(pl.program_id(0) == 0)
    def _():
        out_ref[...] = refs[count][...] if carried else jnp.zeros_like(out_ref)

    for part, partner_ref in enumerate(partners):
        partner = partner_ref[...]
        pair = lax.dot_general(
            own_ref[...], partner, (((1,), (1,)), ((), ())), preferred_element_type=jnp.float32
        )
        amp = (pair / (row_ref[...] + cols_ref[part])).astype(jnp.bfloat16)
        out_ref[...] += jnp.dot(amp, partner, preferred_element_type=jnp.float32)


def pair_step(chunk, own, row, partners, cols, out, total, carried):
    rows, aux = own.shape
    count = partners[0].shape[0]
    width = min(512, count)
    in_specs = [
        pl.BlockSpec((rows, aux), lambda i: (0, 0)),
        pl.BlockSpec((rows, 1), lambda i: (0, 0)),
        pl.BlockSpec((len(partners), 1, width), lambda i: (0, 0, i)),
        *[pl.BlockSpec((width, aux), lambda i: (i, 0)) for _ in partners],
    ]
    operands = [own, row, jnp.stack(cols), *partners]
    aliases = {}
    if out is not None:
        in_specs.append(
            pl.BlockSpec((rows, aux), lambda i: (chunk, 0))
            if carried
            else pl.BlockSpec(memory_space=pl.ANY)
        )
        aliases = {len(operands): 0}
        operands.append(out)
    return pl.pallas_call(
        functools.partial(pair_body, len(partners), carried),
        grid=(count // width,),
        in_specs=in_specs,
        out_specs=pl.BlockSpec((rows, aux), lambda i: (chunk, 0)),
        out_shape=jax.ShapeDtypeStruct((total, aux), jnp.float32),
        input_output_aliases=aliases,
        compiler_params=pltpu.CompilerParams(vmem_limit_bytes=VMEM),
        cost_estimate=pl.CostEstimate(
            flops=4 * rows * count * len(partners) * aux,
            bytes_accessed=2 * count * len(partners) * aux + 6 * rows * aux,
            transcendentals=0,
        ),
        name="pair",
    )(*operands)


def over_chips(value):
    mine = gather_chips(value)
    return mine, swap_cores(mine)


def gather_chips(value):
    size = lax.axis_size("occ")
    groups = [list(range(core, size, 2)) for core in (0, 1)]
    return lax.all_gather(value, "occ", axis=0, tiled=True, axis_index_groups=groups)


def swap_cores(mine):
    size = lax.axis_size("occ")
    return lax.ppermute(mine, "occ", [(i, i + 1 - 2 * (i % 2)) for i in range(size)])


def gather_metric(metric_root):
    rows, aux = metric_root.shape
    column = lax.all_gather(metric_root, "vir", axis=0, tiled=True)
    mine, other = over_chips(column)
    shape = (lax.axis_size("occ") // 2, 1, column.shape[0], aux)
    mine, other = mine.reshape(shape), other.reshape(shape)
    even = lax.rem(lax.axis_index("occ"), 2) == 0
    both = jnp.concatenate(
        [jnp.where(even, mine, other), jnp.where(even, other, mine)], axis=1
    )
    return both.reshape(aux, aux)


def fit(metric, half):
    return jnp.einsum("pr,qp->rq", half, metric, preferred_element_type=jnp.float32).astype(
        jnp.bfloat16
    )


def local(three_index, virt_coeff, metric_root, owner_table, pair_order, occ_energy, vir_energy):
    aux_rows, orbitals, atomic = three_index.shape
    virtuals = virt_coeff.shape[1]
    occ_size = lax.axis_size("occ")
    vir_size = lax.axis_size("vir")
    devices = occ_size * vir_size
    per_dev = orbitals // devices
    group = orbitals // occ_size
    block = virtuals // vir_size
    steps = pair_order.shape[0]
    kept = group // CHUNKS
    per_part = steps // PARTS
    share = per_dev * virtuals // occ_size
    occ_idx = lax.axis_index("occ")
    vir_idx = lax.axis_index("vir")

    one_hot = owner_table[:, None] == jnp.arange(orbitals, dtype=jnp.int32)[None, :]
    eps = jnp.sum(jnp.where(one_hot, occ_energy[None, :], 0.0), axis=1)
    metric = gather_metric(metric_root)
    ordered = half_step(three_index, virt_coeff, one_hot.astype(jnp.bfloat16))

    def exchange(value):
        return lax.all_to_all(value, AXES, split_axis=0, concat_axis=0, tiled=True)

    def after(value, other):
        return lax.optimization_barrier((value, other))

    picked, cols = [], []
    for part in range(PARTS):
        roots = [pair_order[part * per_part + i] for i in range(per_part)]
        wanted = jnp.stack(
            [lax.dynamic_slice_in_dim(ordered, root * group, group, 1) for root in roots], axis=1
        )
        wanted = wanted.reshape(aux_rows, per_part, vir_size, occ_size, share)
        picked.append(wanted.transpose(3, 2, 0, 1, 4).reshape(devices, aux_rows, per_part * share))
        col = []
        for root in roots:
            start = (root * vir_size + vir_idx) * per_dev
            part_eps = lax.dynamic_slice_in_dim(eps, start, per_dev, 0)
            col.append((part_eps[:, None] - vir_energy[None, :]).reshape(occ_size, share))
        col = jnp.stack(col, axis=1).reshape(occ_size // 2, 2, per_part * share)
        core = lax.rem(occ_idx, 2)
        cols.append([jnp.take(col, c, axis=1).reshape(1, -1) for c in (core, 1 - core)])

    own_eps = lax.dynamic_slice_in_dim(eps, occ_idx * group, group, 0)
    block_eps = lax.dynamic_slice_in_dim(vir_energy, vir_idx * block, block, 0)
    row = (own_eps[:, None] - block_eps[None, :]).reshape(CHUNKS, kept * block, 1)
    split = ordered.reshape(aux_rows, occ_size, CHUNKS, kept, vir_size, block)
    split = [
        split[:, :, chunk].transpose(1, 3, 0, 2, 4).reshape(devices, aux_rows, kept * block)
        for chunk in range(CHUNKS)
    ]

    def partner_of(taken):
        mine = fit(metric, taken.reshape(devices * aux_rows, per_part * share))
        return mine, gather_chips(mine)

    def own_of(owned):
        return fit(metric, owned.reshape(devices * aux_rows, kept * block))

    total = group * block
    taken, split, picked[1] = lax.optimization_barrier((exchange(picked[0]), split, picked[1]))
    mine, first = partner_of(taken)
    owned, mine = after(exchange(split[0]), mine)
    own = own_of(owned)
    taken, own = after(exchange(picked[1]), own)
    mine, second = partner_of(taken)
    first = [first, swap_cores(first)]
    out, owns = None, [own]
    early = CHUNKS - 1
    for chunk in range(early):
        if chunk:
            owned, out = after(exchange(split[chunk]), out)
            if chunk == early - 1:
                second, out = after(second, out)
                second = [second, swap_cores(second)]
            owns.append(own_of(owned))
        out = pair_step(chunk, owns[chunk], row[chunk], first, cols[0], out, total, False)
    for chunk in range(early):
        out = pair_step(chunk, owns[chunk], row[chunk], second, cols[1], out, total, True)
    owned, out = after(exchange(split[early]), out)
    own = own_of(owned)
    both = [*first, *second]
    out = pair_step(early, own, row[early], both, [*cols[0], *cols[1]], out, total, False)
    return out.reshape(group, block, out.shape[1])


def solution(mesh):
    placed = (P(AXES, None, None), P(), P(AXES, None), P(), P(), P(), P())
    return jax.shard_map(
        local, mesh=mesh, in_specs=placed, out_specs=P("occ", "vir", None), check_vma=False
    )
```

time: 929 us -> 614 us (0.66)
  waiting for transfers between devices: 577 us -> 178 us
  Pallas kernels: 0 us -> 198 us
  matrix products: 236 us -> 55.4 us
  blocking collectives: 0 us -> 53.2 us
  starting transfers between devices: 15.2 us -> 24.6 us
    all_to_all x2 -> x5, waiting for transfers between devices: 397 us -> 79.4 us  [exchange(): return lax.all_to_all(value, AXES, split_axis=0, concat_axis=0, tiled=True)]
    pallas_call x0 -> x8, Pallas kernels: none -> 198 us  [the longest x7 184 us: pair_step(): pl.pallas_call(functools.partial(pair_body, len(partners), carried), grid...]
    dot_general x11 -> x6, matrix products: 236 us -> 55.4 us  [fit(): jnp.einsum('pr,qp->rq', half, metric, preferred_element_type=jnp.float32)]
    psum x1 -> x0, waiting for transfers between devices: 179 us -> none  [spread(): return lax.psum(kept, axis)]
    all_gather x1 -> x4, waiting for transfers between devices: 0.01 us -> 98.3 us  [the longest x3 66 us: gather_chips(): lax.all_gather(value, 'occ', axis=0, tiled=True, axis_index_groups=groups)]
    all_to_all x0 -> x1, blocking collectives: none -> 53.2 us  [exchange(): return lax.all_to_all(value, AXES, split_axis=0, concat_axis=0, tiled=True)]
    all_to_all x3 -> x0, local copies, waits for them, and re-layouts: 28 us -> none  [the longest x2 20.1 us: local(): lax.all_to_all(fitted, 'vir', split_axis=1, concat_axis=0, tiled=True)]
    reshape x1 -> x9, local copies, waits for them, and re-layouts: 11.4 us -> 31.3 us  [the longest x4 13.3 us: local(): split[:, :, chunk].transpose(1, 3, 0, 2, 4)]
  transfers between devices with their start and end apart: 4 -> 12, of which waited for: 3 -> 6; matrix products, arithmetic and copies ran while one was open for 5% -> 17% of each run, Pallas kernels for 0% -> 26%
where the time goes in v1:
time: 614 us; the launch traced here: 608 us
  Pallas kernels  198 us (32%)
  waiting for transfers between devices  178 us (29%)
  local copies, waits for them, and re-layouts  65.7 us (11%)
  matrix products  55.4 us (9%)
  blocking collectives  53.2 us (9%)
  starting transfers between devices  24.6 us (4%)
  between operations  18.7 us (3%)
  other arithmetic  14.3 us (2%)
    pallas_call x7, Pallas kernels, pair_step(): pl.pallas_call(functools.partial(pair_body, len(partners), carried), grid...  184 us
    all_to_all x5, waiting for transfers between devices, exchange(): return lax.all_to_all(value, AXES, split_axis=0, concat_axis=0, tiled=True)  79.4 us
    all_gather x3, waiting for transfers between devices, gather_chips(): lax.all_gather(value, 'occ', axis=0, tiled=True, axis_index_groups=groups)  66 us
    dot_general x6, matrix products, fit(): jnp.einsum('pr,qp->rq', half, metric, preferred_element_type=jnp.float32)  55.4 us
    all_to_all x1, blocking collectives, exchange(): return lax.all_to_all(value, AXES, split_axis=0, concat_axis=0, tiled=True)  53.2 us
    all_gather x1, waiting for transfers between devices, gather_metric(): column = lax.all_gather(metric_root, 'vir', axis=0, tiled=True)  32.3 us
    all_to_all x5, starting transfers between devices, exchange(): return lax.all_to_all(value, AXES, split_axis=0, concat_axis=0, tiled=True)  23.8 us
    pallas_call x1, Pallas kernels, half_step(): pl.pallas_call(half_body, grid=(aux_rows // rows,), in_specs=[pl.BlockSpe...  14.1 us
  transfers between devices with their start and end apart: 12, of which 6 were waited for; matrix products, arithmetic and copies ran while one was open for 17% of the time, Pallas kernels for 26%

profile of v1, /device:TPU:0, one launch (start us, length us, event | category | flops | bytes accessed | tf_op | source)
XLA Modules:
  0.0 608.1 jit_solution(13099042732323457474)
XLA Ops:
  7.3 32.3 %all-gather.5.cloned.1.call-done = bf16[256,2048]{1,0:T(8,128)(2,1)} async-done(((bf16[64,2048]{1,0:T(8,128)(2,1)}), bf16[256,2048]{1,0:T(8,128)(2,1)}) %all-gather.5.cloned.1.call-update) | async-done | bytes 1048592 | tf_op jit(solution)/shard_map/all_gather | solution.py:127
  39.6 1.5 fusion.4
  43.6 0.7 fusion.perm_ref
  44.4 1.1 copy-done
  45.4 14.1 %half.1 = bf16[64,128,512]{2,1,0:T(8,128)(2,1)} custom-call(bf16[64,128,640]{2,1,0:T(8,128)(2,1)} %x_ref.1, bf16[640,512]{1,0:T(8,128)(2,1)S(1)} %copy-done, bf16[128,128]{1,0:T(8,128)(2,1)S(1)} %fusion.perm_ref), custom_call_target="tpu_custom_call" | custom-call | flops 6442450944 | bytes 18874368 | tf_op jit(solution)/shard_map/half/pallas_call | solution.py:35
  59.5 3.9 constant_dynamic-slice_fusion.1
  63.4 1.2 stack.37
  64.5 1.2 stack.38
  65.7 28.0 %all-gather.7.cloned.1.call-done = bf16[1024,2048]{1,0:T(8,128)(2,1)} async-done(((bf16[256,2048]{1,0:T(8,128)(2,1)}), bf16[1024,2048]{1,0:T(8,128)(2,1)}) %all-gather.7.cloned.1.call-update) | async-done | bytes 4194320 | tf_op jit(solution)/shard_map/all_gather | solution.py:117
  93.7 1.4 maximum_bitcast_fusion
  95.1 2.2 copy.25
  97.3 2.6 reshape.295
  99.9 4.8 all-to-all-start
  105.0 12.6 %reshape.296 = bf16[64,8,4,4,4,128]{5,4,3,2,1,0:T(4,128)(2,1)} reshape(bf16[64,128,512]{2,1,0:T(8,128)(2,1)} %half.1) | data formatting | bytes 16777216 | tf_op jit(solution)/shard_map/reshape | solution.py:191
  118.6 2.2 copy.30
  120.8 2.6 reshape.301
  123.4 9.2 %fusion.1 = (bf16[64,8,1,4,4,128]{5,4,3,2,1,0:T(4,128)(2,1)S(1)}, bf16[64,8,1,4,4,128]{5,4,3,2,1,0:T(4,128)(2,1)S(1)}, bf16[64,8,1,4,4,128]{5,4,3,2,1,0:T(4,128)(2,1)}, bf16[64,8,1,4,4,128]{5,4,3,2,1,0:T(4,128)(2,1)}) fusion(bf16[64,8,4,4,4,128]{5,4,3,2,1,0:T(4,128)(2,1)} %reshape.296), kind=kLoop, calls=%fused_computation.36 | loop fusion | bytes 16777216 | tf_op jit(solution)/shard_map/slice | solution.py:193
  132.6 2.9 copy_bitcast_fusion
  135.5 4.2 reshape.299
  139.6 2.2 reshape.300
  141.9 5.6 copy_bitcast_fusion.2
  147.5 2.7 reshape.297
  150.3 4.2 reshape.298
  154.4 5.3 broadcast_select_fusion.1
  159.7 6.2 %pad_maximum_fusion = bf16[4,2,256,2048]{3,2,1,0:T(8,128)(2,1)} fusion(bf16[4,1,256,2048]{3,2,1,0:T(8,128)(2,1)} %bitcast.59, bf16[4,1,256,2048]{3,2,1,0:T(8,128)(2,1)S(1)} %bitcast.58), kind=kLoop, calls=%fused_computation | loop fusion | flops 4194304 | bytes 16777216 | tf_op jit(solution)/shard_map/concatenate | solution.py:132
  165.9 9.9 %convolution_convert_fusion.5 = bf16[512,2048]{1,0:T(8,128)(2,1)} fusion(bf16[2048,512]{1,0:T(8,128)(2,1)} %bitcast.14, bf16[2048,2048]{1,0:T(8,128)(2,1)} %bitcast.60), kind=kOutput, calls=%fused_computation.8 | convolution fusion | flops 4296015872 | bytes 12582912 | tf_op jit(solution)/shard_map/pr,qp->rq/dot_general | solution.py:139
  175.8 53.2 %all_to_all.30 = bf16[32,64,512]{2,1,0:T(8,128)(2,1)} all-to-all(bf16[32,64,512]{2,1,0:T(8,128)(2,1)S(1)} %reshape.297), channel_id=1, replica_groups=mesh['occ'=8,'vir'=4] {'occ','vir'}, dimensions={0} | all-to-all | bytes 4194304 | tf_op jit(solution)/shard_map/all_to_all | solution.py:166
  229.0 4.7 all-to-all-start.4
  234.2 9.9 %convolution_convert_fusion.4.own_ref = bf16[512,2048]{1,0:T(8,128)(2,1)S(1)} fusion(bf16[2048,512]{1,0:T(8,128)(2,1)} %bitcast.66, bf16[2048,2048]{1,0:T(8,128)(2,1)} %bitcast.61), kind=kOutput, calls=%fused_computation.7 | convolution fusion | flops 4296015872 | bytes 12582912 | tf_op jit(solution)/shard_map/pr,qp->rq/dot_general | solution.py:139
  244.1 36.7 %all-to-all-done.4 = bf16[32,64,512]{2,1,0:T(8,128)(2,1)} async-done(((bf16[32,64,512]{2,1,0:T(8,128)(2,1)}), bf16[32,64,512]{2,1,0:T(8,128)(2,1)}, u32[]{:S(2)}, u32[]{:S(2)}) %all-to-all-start.4) | async-done | bytes 2097184 | tf_op jit(solution)/shard_map/all_to_all | solution.py:166
  280.8 23.4 %all-gather.9.cloned.1.call-done.refs_0_ = bf16[2048,2048]{1,0:T(8,128)(2,1)} async-done(((bf16[512,2048]{1,0:T(8,128)(2,1)}), bf16[2048,2048]{1,0:T(8,128)(2,1)}) %all-gather.9.cloned.1.call-update) | async-done | bytes 8388624 | tf_op jit(solution)/shard_map/all_gather | solution.py:117
  304.3 9.9 %convolution_convert_fusion.1 = bf16[512,2048]{1,0:T(8,128)(2,1)} fusion(bf16[2048,512]{1,0:T(8,128)(2,1)} %bitcast.28, bf16[2048,2048]{1,0:T(8,128)(2,1)} %bitcast.62), kind=kOutput, calls=%fused_computation.4 | convolution fusion | flops 4296015872 | bytes 12582912 | tf_op jit(solution)/shard_map/pr,qp->rq/dot_general | solution.py:139
  314.2 4.8 all-to-all-start.3
  323.4 42.7 %all-to-all-done.3 = bf16[32,64,512]{2,1,0:T(8,128)(2,1)} async-done(((bf16[32,64,512]{2,1,0:T(8,128)(2,1)}), bf16[32,64,512]{2,1,0:T(8,128)(2,1)}, u32[]{:S(2)}, u32[]{:S(2)}) %all-to-all-start.3) | async-done | bytes 2097184 | tf_op jit(solution)/shard_map/all_to_all | solution.py:166
  366.1 4.6 all-to-all-start.2
  370.7 23.2 %pair.7.refs_2_ = f32[2048,2048]{1,0:T(8,128)} custom-call(bf16[512,2048]{1,0:T(8,128)(2,1)S(1)} %convolution_convert_fusion.4.own_ref, f32[512,1]{1,0:T(8,128)S(1)} %copy.31.row_ref, f32[2,1,2048]{2,1,0:T(1,128)S(1)} %pad_maximum_fusion.3.cols_ref, bf16[2048,2048]{1,0:T(8,128)(2,1)} %all-gather.9.cloned.1.call-done.refs_0_, ...), custom_call_target="tpu_custom_call" | custom-call | flops 17179869184 | bytes 23068672 | tf_op jit(solution)/shard_map/pair/pallas_call | solution.py:92
  394.0 8.6 %convolution_convert_fusion.3.own_ref = bf16[512,2048]{1,0:T(8,128)(2,1)S(1)} fusion(bf16[2048,512]{1,0:T(8,128)(2,1)} %bitcast.22, bf16[2048,2048]{1,0:T(8,128)(2,1)} %bitcast.63), kind=kOutput, calls=%fused_computation.6 | convolution fusion | flops 4296015872 | bytes 12582912 | tf_op jit(solution)/shard_map/pr,qp->rq/dot_general | solution.py:139
  402.5 22.8 %pair.8.refs_2_ = f32[2048,2048]{1,0:T(8,128)} custom-call(bf16[512,2048]{1,0:T(8,128)(2,1)S(1)} %convolution_convert_fusion.3.own_ref, f32[512,1]{1,0:T(8,128)S(1)} %copy.32.row_ref, f32[2,1,2048]{2,1,0:T(1,128)S(1)} %pad_maximum_fusion.3.cols_ref, bf16[2048,2048]{1,0:T(8,128)(2,1)} %all-gather.9.cloned.1.call-done.refs_0_, ...), custom_call_target="tpu_custom_call", output_to_operand_aliasing={{}: (5, {})} | custom-call | flops 17179869184 | bytes 23068672 | tf_op jit(solution)/shard_map/pair/pallas_call | solution.py:92
  425.4 1.4 copy-done.1
  426.7 14.6 %all-gather.11.cloned.1.call-done.refs_0_.refs_2_ = bf16[2048,2048]{1,0:T(8,128)(2,1)} async-done(((bf16[512,2048]{1,0:T(8,128)(2,1)}), bf16[2048,2048]{1,0:T(8,128)(2,1)}) %all-gather.11.cloned.1.call-update) | async-done | bytes 8388624 | tf_op jit(solution)/shard_map/all_gather | solution.py:117
  441.8 4.9 all-to-all-start.1
  446.7 8.6 %convolution_convert_fusion.2.own_ref = bf16[512,2048]{1,0:T(8,128)(2,1)S(1)} fusion(bf16[2048,512]{1,0:T(8,128)(2,1)} %bitcast.24, bf16[2048,2048]{1,0:T(8,128)(2,1)} %bitcast.64), kind=kOutput, calls=%fused_computation.5 | convolution fusion | flops 4296015872 | bytes 12582912 | tf_op jit(solution)/shard_map/pr,qp->rq/dot_general | solution.py:139
  455.3 22.8 %pair.9.refs_2_ = f32[2048,2048]{1,0:T(8,128)} custom-call(bf16[512,2048]{1,0:T(8,128)(2,1)S(1)} %convolution_convert_fusion.2.own_ref, f32[512,1]{1,0:T(8,128)S(1)} %copy.36.row_ref, f32[2,1,2048]{2,1,0:T(1,128)S(1)} %pad_maximum_fusion.3.cols_ref, bf16[2048,2048]{1,0:T(8,128)(2,1)} %all-gather.9.cloned.1.call-done.refs_0_, ...), custom_call_target="tpu_custom_call", output_to_operand_aliasing={{}: (5, {})} | custom-call | flops 17179869184 | bytes 23068672 | tf_op jit(solution)/shard_map/pair/pallas_call | solution.py:92
  478.1 24.6 %pair.10.refs_2_ = f32[2048,2048]{1,0:T(8,128)} custom-call(bf16[512,2048]{1,0:T(8,128)(2,1)S(1)} %convolution_convert_fusion.4.own_ref, f32[512,1]{1,0:T(8,128)S(1)} %copy.31.row_ref, f32[2,1,2048]{2,1,0:T(1,128)S(1)} %pad_maximum_fusion.5.cols_ref, ...), custom_call_target="tpu_custom_call", output_to_operand_aliasing={{}: (5, {})} | custom-call | flops 17179869184 | bytes 23068672 | tf_op jit(solution)/shard_map/pair/pallas_call | solution.py:92
  502.7 24.0 %pair.11.refs_2_ = f32[2048,2048]{1,0:T(8,128)} custom-call(bf16[512,2048]{1,0:T(8,128)(2,1)S(1)} %copy-done.2, f32[512,1]{1,0:T(8,128)S(1)} %copy.32.row_ref, f32[2,1,2048]{2,1,0:T(1,128)S(1)} %pad_maximum_fusion.5.cols_ref, bf16[2048,2048]{1,0:T(8,128)(2,1)} %all-gather.11.cloned.1.call-done.refs_0_.refs_2_, ...), custom_call_target="tpu_custom_call", output_to_operand_aliasing={{}: (5, {})} | custom-call | flops 17179869184 | bytes 23068672 | tf_op jit(solution)/shard_map/pair/pallas_call | solution.py:92
  526.8 24.2 %pair.12.refs_4_ = f32[2048,2048]{1,0:T(8,128)} custom-call(bf16[512,2048]{1,0:T(8,128)(2,1)S(1)} %convolution_convert_fusion.2.own_ref, f32[512,1]{1,0:T(8,128)S(1)} %copy.36.row_ref, f32[2,1,2048]{2,1,0:T(1,128)S(1)} %pad_maximum_fusion.5.cols_ref, ...), custom_call_target="tpu_custom_call", output_to_operand_aliasing={{}: (5, {})} | custom-call | flops 17179869184 | bytes 23068672 | tf_op jit(solution)/shard_map/pair/pallas_call | solution.py:92
  551.0 8.6 %convolution_convert_fusion.own_ref = bf16[512,2048]{1,0:T(8,128)(2,1)S(1)} fusion(bf16[2048,512]{1,0:T(8,128)(2,1)} %bitcast.29, bf16[2048,2048]{1,0:T(8,128)(2,1)} %bitcast.65), kind=kOutput, calls=%fused_computation.3 | convolution fusion | flops 4296015872 | bytes 12582912 | tf_op jit(solution)/shard_map/pr,qp->rq/dot_general | solution.py:139
  559.6 41.8 %pair.13 = f32[2048,2048]{1,0:T(8,128)} custom-call(bf16[512,2048]{1,0:T(8,128)(2,1)S(1)} %convolution_convert_fusion.own_ref, f32[512,1]{1,0:T(8,128)S(1)} %copy.37.row_ref, f32[4,1,2048]{2,1,0:T(1,128)S(1)} %pad_maximum_fusion.1.cols_ref, bf16[2048,2048]{1,0:T(8,128)(2,1)} %all-gather.9.cloned.1.call-done.refs_0_, ...), custom_call_target="tpu_custom_call", output_to_operand_aliasing={{}: (7, {})} | custom-call | flops 34359738368 | bytes 39845888 | tf_op jit(solution)/shard_map/pair/pallas_call | solution.py:92
  (64 shorter events, 4.6 us)
Async XLA Ops:
  6.5 33.1 %all-gather.5.cloned.1.call-start = ((), (), s32[]{:S(2)}) async-start(), calls=%async_computation.6 | async-start | bytes 1310720 | tf_op jit(solution)/shard_map/all_gather | solution.py:127
  7.3 86.4 %all-gather.7.cloned.1.call-start = ((), (), s32[]{:S(2)}) async-start(), calls=%async_computation.7 | async-start | bytes 5242880 | tf_op jit(solution)/shard_map/all_gather | solution.py:117
  44.4 1.1 copy-start
  64.5 29.1 %copy-start.4 = (bf16[64,1,4,8,256]{4,3,2,0,1:T(8,128)(2,1)S(1)}, bf16[64,1,4,8,256]{4,3,2,0,1:T(8,128)(2,1)}, u32[]{:S(2)}) copy-start(bf16[64,1,4,8,256]{4,3,2,0,1:T(8,128)(2,1)} %stack.37) | copy-start | bytes 3145732
  93.7 60.8 %collective-permute-start = (bf16[1024,2048]{1,0:T(8,128)(2,1)}, bf16[1024,2048]{1,0:T(8,128)(2,1)}, u32[]{:S(2)}, u32[]{:S(2)}) collective-permute-start(bf16[1024,2048]{1,0:T(8,128)(2,1)} %all-gather.7.cloned.1.call-done), channel_id=1, source_target_pairs={{0,4},{4,0},{8,12},{12,8},{16,20},{20,16},{24,28},{28,24},{1,5},{5... | collective-permute-start | bytes 12582920 | tf_op jit(solution)/shard_map/ppermute | solution.py:122
  99.9 54.5 %all-to-all-start = ((bf16[32,64,512]{2,1,0:T(8,128)(2,1)}), bf16[32,64,512]{2,1,0:T(8,128)(2,1)}, u32[]{:S(2)}, u32[]{:S(2)}) async-start(bf16[32,64,512]{2,1,0:T(8,128)(2,1)} %reshape.295), calls=%async_computation | async-start | bytes 4194304 | tf_op jit(solution)/shard_map/all_to_all | solution.py:166
  104.7 12.9 %copy-start.3 = (bf16[64,16,512]{2,1,0:T(8,128)(2,1)S(1)}, bf16[64,16,512]{2,1,0:T(8,128)(2,1)}, u32[]{:S(2)}) copy-start(bf16[64,16,512]{2,1,0:T(8,128)(2,1)} %get-tuple-element.53) | copy-start | bytes 3145732
  104.8 199.5 %all-gather.9.cloned.1.call-start = ((), (), s32[]{:S(2)}) async-start(), calls=%async_computation.8 | async-start | bytes 10485760 | tf_op jit(solution)/shard_map/all_gather | solution.py:117
  229.0 51.8 %all-to-all-start.4 = ((bf16[32,64,512]{2,1,0:T(8,128)(2,1)}), bf16[32,64,512]{2,1,0:T(8,128)(2,1)}, u32[]{:S(2)}, u32[]{:S(2)}) async-start(bf16[32,64,512]{2,1,0:T(8,128)(2,1)} %reshape.301), calls=%async_computation.4 | async-start | bytes 4194304 | tf_op jit(solution)/shard_map/all_to_all | solution.py:166
  233.7 207.6 %all-gather.11.cloned.1.call-start = ((), (), s32[]{:S(2)}) async-start(), calls=%async_computation.9 | async-start | bytes 10485760 | tf_op jit(solution)/shard_map/all_gather | solution.py:117
  304.2 66.5 %collective-permute-start.1 = (bf16[2048,2048]{1,0:T(8,128)(2,1)}, bf16[2048,2048]{1,0:T(8,128)(2,1)}, u32[]{:S(2)}, u32[]{:S(2)}) collective-permute-start(bf16[2048,2048]{1,0:T(8,128)(2,1)} %all-gather.9.cloned.1.call-done.refs_0_), channel_id=1, source_target_pairs={{0,4},{4,0},{8,12},{12,8},{16,20},{20,16},{24,28},{28,24},{1,5},{5... | collective-permute-start | bytes 25165832 | tf_op jit(solution)/shard_map/ppermute | solution.py:122
  314.2 7.4 %copy-start.6 = (s32[128]{0:T(128)S(1)}, s32[128]{0:T(128)}, u32[]{:S(2)}) copy-start(s32[128]{0:T(128)} %param.12) | copy-start | bytes 1540
  314.2 7.4 %copy-start.7 = (f32[128]{0:T(128)S(1)}, f32[128]{0:T(128)}, u32[]{:S(2)}) copy-start(f32[128]{0:T(128)} %param.14) | copy-start | bytes 1540
  314.2 8.3 %copy-start.5 = (f32[512]{0:T(512)S(1)}, f32[512]{0:T(512)}, u32[]{:S(2)}) copy-start(f32[512]{0:T(512)} %param.15) | copy-start | bytes 6148
  314.2 51.9 %all-to-all-start.3 = ((bf16[32,64,512]{2,1,0:T(8,128)(2,1)}), bf16[32,64,512]{2,1,0:T(8,128)(2,1)}, u32[]{:S(2)}, u32[]{:S(2)}) async-start(bf16[32,64,512]{2,1,0:T(8,128)(2,1)} %reshape.298), calls=%async_computation.3 | async-start | bytes 4194304 | tf_op jit(solution)/shard_map/all_to_all | solution.py:166
  366.1 60.6 %all-to-all-start.2 = ((bf16[32,64,512]{2,1,0:T(8,128)(2,1)}), bf16[32,64,512]{2,1,0:T(8,128)(2,1)}, u32[]{:S(2)}, u32[]{:S(2)}) async-start(bf16[32,64,512]{2,1,0:T(8,128)(2,1)} %reshape.299), calls=%async_computation.2 | async-start | bytes 4194304 | tf_op jit(solution)/shard_map/all_to_all | solution.py:166
  425.4 1.4 copy-start.1
  441.4 36.7 %collective-permute-start.2 = (bf16[2048,2048]{1,0:T(8,128)(2,1)}, bf16[2048,2048]{1,0:T(8,128)(2,1)}, u32[]{:S(2)}, u32[]{:S(2)}) collective-permute-start(bf16[2048,2048]{1,0:T(8,128)(2,1)} %all-gather.11.cloned.1.call-done.refs_0_.refs_2_), channel_id=1, source_target_pairs={{0,4},{4,0},{8,12},{12,8},{16,20},{20,16},{24,28},{28,24},{1,5},{5... | collective-permute-start | bytes 25165832 | tf_op jit(solution)/shard_map/ppermute | solution.py:122
  441.8 109.2 %all-to-all-start.1 = ((bf16[32,64,512]{2,1,0:T(8,128)(2,1)}), bf16[32,64,512]{2,1,0:T(8,128)(2,1)}, u32[]{:S(2)}, u32[]{:S(2)}) async-start(bf16[32,64,512]{2,1,0:T(8,128)(2,1)} %reshape.300), calls=%async_computation.1 | async-start | bytes 4194304 | tf_op jit(solution)/shard_map/all_to_all | solution.py:166
  478.1 24.7 %copy-start.2 = (bf16[512,2048]{1,0:T(8,128)(2,1)S(1)}, bf16[512,2048]{1,0:T(8,128)(2,1)}, u32[]{:S(2)}) copy-start(bf16[512,2048]{1,0:T(8,128)(2,1)} %copy-done.1) | copy-start | bytes 6291460
Sparse Core Ops, SparseCore 0:
  8.9 30.6 all-gather.4
  41.4 52.1 all-gather.6
  175.9 128.2 all-gather.8
  314.3 126.9 all-gather.10
